TPU v7x, 512 devices: a whole 4x8x8 slice. The times are simulated.
512 devices in a mesh: seq: 64 (over y, x, core), chan: 8 (over z).
Axes of the slice: x: 4, y: 8, z: 8, core: 2. Of those that a mesh axis runs over, the one named last changes fastest.
Arguments:
- hidden_in: bfloat16 [8192, 8192], P('seq', 'chan'), as said below
- query_mr: bfloat16 [8192, 8192], P('seq', 'chan'), may hold values from -6 to 6
- key_mr: bfloat16 [8192, 8192], P('seq', 'chan'), may hold values from -6 to 6
- value_mr: bfloat16 [8192, 8192], P('seq', 'chan'), may hold values from -6 to 6
- query_li: bfloat16 [8192, 8192], P('seq', 'chan'), may hold values from -6 to 6
- key_li: bfloat16 [8192, 8192], P('seq', 'chan'), may hold values from -6 to 6
- mr_filter: bfloat16 [128, 512], P(None, 'chan'), may hold values from -0.5 to 0.5
- li_rate: float32 [16, 8192], P(None, 'chan'), as said below
- li_residue: float32 [16, 8192], P(None, 'chan'), may hold values from -4 to 4
- norm_gain: float32 [8192], P('chan'), may hold values from 0.25 to 1.75
Outputs:
- normed_out: bfloat16 [8192, 8192], P('seq', 'chan')
Inputs may be any that keep to these rules, and one draw needn't show every extreme that they name: `hidden_in`: real values of moderate size. `li_rate`: decay rates per position, all positive, from 1 / 81920 to 1 / 30.
All inputs are finite; a program needn't handle non-finite values.
Results may differ from a plain program's by a relative error of at most 0.0055.
Values may be sent and summed in bfloat16 or wider, within the bound.
No kernel may reach another device: no remote copies, remote signals or barrier semaphores. Data moves between devices by JAX's collectives and lax.ppermute only.
A program may use at most 64 MiB of HBM per device.

v0:
```python
import jax
import jax.numpy as jnp
from jax import lax
from jax.sharding import PartitionSpec as P


def passed_along(block, axis, distance):
    devices = range(lax.axis_size(axis))
    route = [(i - distance, i) for i in devices if i - distance in devices]
    return lax.ppermute(block, axis, route)


def band_matrix(filter_taps, filter_len):
    group_count = filter_taps.shape[1]
    padded = jnp.concatenate(
        [
            jnp.zeros((1, group_count), filter_taps.dtype),
            jnp.flip(filter_taps, 0),
            jnp.zeros((filter_len, group_count), filter_taps.dtype),
        ],
        0,
    )
    repeated = jnp.tile(padded, (filter_len, 1))[: filter_len * 2 * filter_len]
    return repeated.reshape(filter_len, 2 * filter_len, group_count)


def band_apply(toeplitz, earlier, latter, group_count):
    rows, channels = earlier.shape
    filter_len = toeplitz.shape[0]
    blocks = rows // filter_len
    earlier_rows = earlier.reshape(blocks, filter_len, group_count, channels // group_count)
    latter_rows = latter.reshape(blocks, filter_len, group_count, channels // group_count)
    windows = jnp.concatenate([earlier_rows, latter_rows], 1)
    result = jnp.einsum("tsg,bsgk->btgk", toeplitz, windows, preferred_element_type=jnp.float32)
    return result.reshape(rows, channels)


def per_device(
    hidden_in,
    query_mr,
    key_mr,
    value_mr,
    query_li,
    key_li,
    mr_filter,
    li_rate,
    li_residue,
    norm_gain,
):
    tokens, channels = key_mr.shape
    filter_len = mr_filter.shape[0]
    group_count = mr_filter.shape[1]
    highest = lax.Precision.HIGHEST
    product = (key_mr.astype(jnp.float32) * value_mr.astype(jnp.float32)).astype(jnp.bfloat16)
    toeplitz = band_matrix(mr_filter, filter_len)
    prior_rows = passed_along(product[tokens - filter_len + 1 :], "seq", 1)
    first_earlier = jnp.concatenate([jnp.zeros((1, channels), jnp.bfloat16), prior_rows], 0)
    earlier_all = jnp.concatenate([first_earlier, product[: tokens - filter_len]], 0)
    conv_mr = band_apply(toeplitz, earlier_all, product, group_count)
    out_mr = (query_mr.astype(jnp.float32) * conv_mr).astype(jnp.bfloat16)
    source = key_li.astype(jnp.float32) * out_mr.astype(jnp.float32)
    block_len = 16
    block_count = tokens // block_len
    scaled = li_residue * jnp.sqrt(-jnp.expm1(-2.0 * li_rate))
    lag_steps = jnp.arange(block_len).astype(jnp.float32)
    mode_taps = jnp.sum(scaled[None] * jnp.exp(-lag_steps[:, None, None] * li_rate[None]), 1)
    lag_index = jnp.arange(block_len)
    lag_grid = lag_index[:, None] - lag_index[None, :]
    selector = (lag_grid[:, :, None] == lag_index[None, None, :]).astype(jnp.float32)
    intra_block = jnp.einsum("tsd,dc->tsc", selector, mode_taps, precision=highest)
    decay_out = jnp.exp(-(block_len - 1 - lag_steps)[:, None, None] * li_rate[None])
    decay_in = scaled[None] * jnp.exp(-(lag_steps + 1.0)[:, None, None] * li_rate[None])
    blocks_in = source.reshape(block_count, block_len, channels)
    local_part = jnp.einsum("tsc,bsc->btc", intra_block, blocks_in, precision=highest)
    block_ends = jnp.einsum("snc,bsc->bnc", decay_out, blocks_in, precision=highest)
    block_decay = jnp.exp(-block_len * li_rate)

    def combine_blocks(earlier, latter):
        return (earlier[0] * latter[0], latter[0] * earlier[1] + latter[1])

    _, inclusive = lax.associative_scan(
        combine_blocks, (jnp.broadcast_to(block_decay[None], block_ends.shape), block_ends), axis=0
    )
    position = lax.axis_index("seq")
    shard_rows = lax.all_gather(inclusive[-1:], "seq", axis=0, tiled=True)
    owners = jnp.arange(shard_rows.shape[0], dtype=jnp.int32)
    distance = jnp.maximum(position - 1 - owners, 0).astype(jnp.float32)
    weight = jnp.where(
        (owners < position)[:, None, None],
        jnp.exp(-(tokens * distance)[:, None, None] * li_rate[None]),
        0.0,
    )
    incoming = jnp.sum(weight * shard_rows, 0)
    offsets = jnp.arange(block_count).astype(jnp.float32) * block_len
    start_states = (
        jnp.concatenate([jnp.zeros_like(inclusive[:1]), inclusive[:-1]], 0)
        + jnp.exp(-offsets[:, None, None] * li_rate[None]) * incoming[None]
    )
    from_states = jnp.einsum("tnc,bnc->btc", decay_in, start_states, precision=highest)
    conv_li = (local_part + from_states).reshape(tokens, channels)
    combined = (
        hidden_in.astype(jnp.float32)
        + out_mr.astype(jnp.float32)
        + query_li.astype(jnp.float32) * conv_li
    )
    local_squares = jnp.sum(combined * combined, axis=1)
    square_sum = lax.psum(local_squares, "chan")
    inverse_rms = lax.rsqrt(square_sum / (channels * lax.axis_size("chan")) + 1e-06)
    return (combined * inverse_rms[:, None] * norm_gain[None, :]).astype(jnp.bfloat16)


def solution(mesh):
    in_specs = (
        P("seq", "chan"),
        P("seq", "chan"),
        P("seq", "chan"),
        P("seq", "chan"),
        P("seq", "chan"),
        P("seq", "chan"),
        P(None, "chan"),
        P(None, "chan"),
        P(None, "chan"),
        P("chan"),
    )
    out_specs = P("seq", "chan")
    return jax.shard_map(
        per_device, mesh=mesh, in_specs=in_specs, out_specs=out_specs, check_vma=False
    )
```

profile of v0, /device:TPU:16, one launch (start us, length us, event | category | flops | bytes accessed | tf_op | source)
XLA Modules:
  0.0 193.9 jit_solution(13816346787504282258)
XLA Ops:
  6.5 0.0 all-gather.2.cloned.1.call-start
  6.5 1.1 multiply_convert_fusion.2
  7.6 0.1 slice.90
  7.7 1.9 collective-permute-start
  9.6 0.8 rev.4
  10.4 0.1 pad.34.clone
  10.5 0.1 maximum_maximum_fusion
  10.6 0.2 copy.99
  10.8 3.2 %tile.4 = bf16[128,257,64]{1,0,2:T(8,128)(2,1)} broadcast(bf16[257,64]{0,1:T(8,128)(2,1)S(1)} %maximum_maximum_fusion), dimensions={1,2} | broadcast | bytes 4243584 | tf_op jit(solution)/shard_map/tile | solution.py:23
  14.0 10.8 %tile.10 = bf16[32896,64]{0,1:T(8,128)(2,1)} reshape(bf16[128,257,64]{1,0,2:T(8,128)(2,1)} %tile.4) | data formatting | bytes 8421376 | tf_op jit(solution)/shard_map/tile | solution.py:23
  24.8 0.0 slice-start
  24.8 2.2 %slice-done = bf16[32768,64]{0,1:T(8,128)(2,1)S(1)} async-done(((bf16[32896,64]{0,1:T(8,128)(2,1)}), bf16[32768,64]{0,1:T(8,128)(2,1)S(1)}, s32[]{:S(2)}) %slice-start) | async-done | bytes 4194328 | tf_op jit(solution)/shard_map/slice | solution.py:23
  27.0 0.0 copy-start
  27.0 0.0 copy-start.6
  27.0 3.0 %copy.113 = bf16[8,8,128,256]{3,2,1,0:T(8,128)(2,1)} copy(bf16[8,8,128,256]{3,1,2,0:T(8,128)(2,1)S(1)} %bitcast.43) | data formatting | bytes 8388608
  30.1 0.0 copy-done
  30.1 0.0 copy-start.4
  30.1 0.0 copy-start.5
  30.1 0.2 copy.102
  30.3 0.0 copy-done.6
  30.3 0.1 fusion.26
  30.4 0.0 collective-permute-done
  30.4 0.2 copy.112
  30.5 0.1 concatenate.18.clone
  30.7 3.4 %fusion.15 = f32[64,16,128]{2,1,0:T(8,128)S(1)} fusion(bf16[128,256,64]{1,0,2:T(8,128)(2,1)} %bitcast.44, bf16[1,128,64,16]{1,3,2,0:T(8,128)(2,1)S(1)} %bitcast.51, bf16[1,128,64,16]{1,3,2,0:T(8,128)(2,1)S(1)} %bitcast.50), kind=kOutput, calls=%fused_computation.19 | convolution fusion | flops 68157440 | bytes 5242880 | tf_op jit(solution)/shard_map/tsg,bsgk->btgk/dot_general | solution.py:34
  34.1 0.2 copy.100
  34.3 0.0 copy-done.4
  34.3 0.0 copy-done.5
  34.3 0.1 convert_multiply_fusion
  34.4 2.6 %copy.104 = f32[8,16,1024]{1,0,2:T(8,128)} copy(f32[8,16,1024]{2,1,0:T(8,128)S(1)} %bitcast.48) | data formatting | bytes 1048576 | tf_op jit(solution)/shard_map/reshape | solution.py:73
  37.1 11.1 %fusion.4 = f32[1024,8,16]{2,1,0:T(8,128)} fusion(f32[8,16,1024]{1,0,2:T(8,128)} %copy.104, f32[16]{0:T(128)S(1)} %subtract_negate_fusion, f32[16,1024]{0,1:T(8,128)S(1)} %copy.102), kind=kOutput, calls=%fused_computation.4 | convolution fusion | flops 25427968 | bytes 1114176 | tf_op jit(solution)/shard_map/snc,bsc->bnc/dot_general | solution.py:75
  48.1 2.8 %copy.107 = f32[1024,8,16]{0,2,1:T(8,128)S(1)} copy(f32[1024,8,16]{2,1,0:T(8,128)} %fusion.4) | data formatting | bytes 1048576 | tf_op jit(solution)/shard_map/snc,bsc->bnc/dot_general | solution.py:75
  51.2 0.0 copy-start.1
  51.2 0.1 pad.65
  51.3 0.6 slice.129
  51.9 0.0 all-gather.2.cloned.1.call-update
  52.0 0.0 copy-done.1
  52.0 0.2 copy.101
  52.2 3.5 %multiply_reduce_fusion = f32[16,1024]{0,1:T(8,128)S(1)} fusion(f32[16,1024]{0,1:T(8,128)S(1)} %copy.102, f32[16]{0:T(128)S(1)} %convert_negate_fusion, f32[16,1024]{0,1:T(8,128)S(1)} %copy.101), kind=kLoop, calls=%fused_computation.7 | loop fusion | flops 770048 | bytes 196672 | tf_op jit(solution)/shard_map/reduce_sum | solution.py:66
  55.7 0.6 fusion.18
  56.3 6.2 %copy.105 = f32[16,16,1024]{1,0,2:T(8,128)} copy(f32[16,16,1024]{2,1,0:T(8,128)S(1)} %fusion.18) | data formatting | bytes 2097152 | tf_op jit(solution)/shard_map/tsd,dc->tsc/dot_general | solution.py:70
  62.5 0.2 pad.26
  62.8 1.0 fusion.20
  63.8 0.1 pad.25
  63.9 0.1 slice_add_fusion
  63.9 17.5 %fusion.29 = f32[1024,8,16]{2,1,0:T(8,128)} fusion(f32[8,16,1024]{1,0,2:T(8,128)} %copy.104, f32[16,16,1024]{1,0,2:T(8,128)} %copy.105), kind=kOutput, calls=%fused_computation.62 | convolution fusion | flops 25165824 | bytes 2097152 | tf_op jit(solution)/shard_map/tsc,bsc->btc/dot_general | solution.py:74
  81.4 60.2 %all-gather.2.cloned.1.call-done = f32[64,16,1024]{2,1,0:T(8,128)} async-done(((f32[1,16,1024]{2,1,0:T(8,128)}), f32[64,16,1024]{2,1,0:T(8,128)}) %all-gather.2.cloned.1.call-update) | async-done | bytes 4194320 | tf_op jit(solution)/shard_map/all_gather | solution.py:85
  141.6 3.1 %multiply_reduce_fusion.1 = f32[16,1024]{1,0:T(8,128)S(1)} fusion(f32[64,16,1024]{2,1,0:T(8,128)} %all-gather.2.cloned.1.call-done, f32[16,1024]{1,0:T(8,128)S(1)} %copy-done, f32[64]{0:T(128)S(1)} %multiply_negate_fusion, pred[64]{0:T(512)(128)(4,1)S(1)} %iota_compare_fusion.2), kind=kLoop, calls=%fused_computation.10 | loop fusion | flops 4177920 | bytes 4325696 | tf_op jit(solution)/shard_map/reduce_sum | solution.py:93
  144.7 0.2 multiply_add_fusion
  144.9 2.6 %copy.108 = f32[8,16,1024]{1,0,2:T(8,128)} copy(f32[8,16,1024]{2,1,0:T(8,128)S(1)} %multiply_add_fusion) | data formatting | bytes 1048576 | tf_op jit(solution)/shard_map/add | solution.py:96
  147.5 17.5 %add_bitcast_fusion = f32[8,16,1024]{1,0,2:T(8,128)} fusion(f32[1024,8,16]{2,1,0:T(8,128)} %fusion.29, f32[8,16,1024]{1,0,2:T(8,128)} %copy.108, f32[16]{0:T(128)S(1)} %add_negate_fusion, f32[16,1024]{0,1:T(8,128)S(1)} %copy.102, f32[16,1024]{0,1:T(8,128)S(1)} %copy.101), kind=kOutput, calls=%fused_computation.8 | convolution fusion | flops 25821184 | bytes 1704000 | tf_op jit(solution)/shard_map/tnc,bnc->btc/dot_general | solution.py:99
  165.0 0.0 copy-start.2
  165.0 0.0 copy-start.3
  165.0 0.0 copy-start.7
  165.0 2.9 %copy.109 = f32[8,16,1024]{2,1,0:T(8,128)S(1)} copy(f32[8,16,1024]{1,0,2:T(8,128)} %add_bitcast_fusion) | data formatting | bytes 1048576 | tf_op jit(solution)/shard_map/add | solution.py:100
  167.8 0.0 copy-done.2
  167.9 0.0 copy-done.3
  167.9 0.2 multiply_reduce_fusion.2
  168.1 18.1 %psum.7 = f32[128]{0:T(128)S(1)} all-reduce(f32[128]{0:T(128)S(1)} %multiply_reduce_fusion.2), channel_id=1, replica_groups=mesh['seq'=64,'chan'=8] {'chan'}, use_global_device_ids=true, to_apply=%region_3.4 | all-reduce | flops 128 | bytes 1024 | tf_op jit(solution)/shard_map/psum | solution.py:107
  186.2 0.0 copy-done.7
  186.2 0.9 multiply_convert_fusion
  (21 shorter events, 0.3 us)
Async XLA Ops:
  6.5 135.0 %all-gather.2.cloned.1.call-start = ((), (), s32[]{:S(2)}) async-start(), calls=%async_computation | async-start | bytes 4259840 | tf_op jit(solution)/shard_map/all_gather | solution.py:85
  7.7 22.6 %collective-permute-start = (bf16[127,1024]{1,0:T(8,128)(2,1)S(1)}, bf16[127,1024]{1,0:T(8,128)(2,1)S(1)}, u32[]{:S(2)}, u32[]{:S(2)}) collective-permute-start(bf16[127,1024]{1,0:T(8,128)(2,1)S(1)} %slice.90), channel_id=1, source_target_pairs={{0,8},{8,16},{16,24},{24,32},{32,40},{40,48},{48,56},{56,64},{64,7... | collective-permute-start | bytes 780296 | tf_op jit(solution)/shard_map/ppermute | solution.py:10
  24.8 2.2 %slice-start = ((bf16[32896,64]{0,1:T(8,128)(2,1)}), bf16[32768,64]{0,1:T(8,128)(2,1)S(1)}, s32[]{:S(2)}) async-start(bf16[32896,64]{0,1:T(8,128)(2,1)} %tile.10), calls=%async_computation.1 | async-start | bytes 8388608 | tf_op jit(solution)/shard_map/slice | solution.py:23
  27.0 3.0 %copy-start = (f32[16,1024]{1,0:T(8,128)S(1)}, f32[16,1024]{1,0:T(8,128)}, u32[]{:S(2)}) copy-start(f32[16,1024]{1,0:T(8,128)} %param.17) | copy-start | bytes 196612
  27.0 3.2 %copy-start.6 = (f32[16,1024]{1,0:T(8,128)S(1)}, f32[16,1024]{1,0:T(8,128)}, u32[]{:S(2)}) copy-start(f32[16,1024]{1,0:T(8,128)} %param.18) | copy-start | bytes 196612
  30.1 4.2 %copy-start.4 = (bf16[128,1024]{1,0:T(8,128)(2,1)S(1)}, bf16[128,1024]{1,0:T(8,128)(2,1)}, u32[]{:S(2)}) copy-start(bf16[128,1024]{1,0:T(8,128)(2,1)} %param.15) | copy-start | bytes 786436
  30.1 4.2 %copy-start.5 = (bf16[128,1024]{1,0:T(8,128)(2,1)S(1)}, bf16[128,1024]{1,0:T(8,128)(2,1)}, u32[]{:S(2)}) copy-start(bf16[128,1024]{1,0:T(8,128)(2,1)} %param.11) | copy-start | bytes 786436
  51.2 0.8 copy-start.1
  165.0 2.9 %copy-start.2 = (bf16[128,1024]{1,0:T(8,128)(2,1)S(1)}, bf16[128,1024]{1,0:T(8,128)(2,1)}, u32[]{:S(2)}) copy-start(bf16[128,1024]{1,0:T(8,128)(2,1)} %param.14) | copy-start | bytes 786436
  165.0 2.9 %copy-start.3 = (bf16[128,1024]{1,0:T(8,128)(2,1)S(1)}, bf16[128,1024]{1,0:T(8,128)(2,1)}, u32[]{:S(2)}) copy-start(bf16[128,1024]{1,0:T(8,128)(2,1)} %param.10) | copy-start | bytes 786436
  165.0 21.2 %copy-start.7 = (f32[1024]{0:T(1024)S(1)}, f32[1024]{0:T(1024)}, u32[]{:S(2)}) copy-start(f32[1024]{0:T(1024)} %param.19) | copy-start | bytes 12292
Sparse Core Ops, SparseCore 0:
  52.1 89.4 all-gather.1
where the time goes:
time: 194 us
  waiting for transfers between devices  60.2 us (31%)
  matrix products  50 us (26%)
  local copies, waits for them, and re-layouts  39.5 us (20%)
  blocking collectives  18.1 us (9%)
  between operations  13.7 us (7%)
  other arithmetic  10.4 us (5%)
    all_gather x1, waiting for transfers between devices, per_device(): shard_rows = lax.all_gather(inclusive[-1:], 'seq', axis=0, tiled=True)  60.2 us
    psum x1, blocking collectives, per_device(): square_sum = lax.psum(local_squares, 'chan')  18.1 us
    dot_general x1, matrix products, per_device(): jnp.einsum('tnc,bnc->btc', decay_in, start_states, precision=highest)  17.5 us
    dot_general x1, matrix products, per_device(): jnp.einsum('tsc,bsc->btc', intra_block, blocks_in, precision=highest)  17.5 us
    another operation x2, local copies, waits for them, and re-layouts, band_matrix(): repeated = jnp.tile(padded, (filter_len, 1))[:filter_len * 2 * filter_len]  14 us
    dot_general x1, matrix products, per_device(): jnp.einsum('snc,bsc->bnc', decay_out, blocks_in, precision=highest)  11.1 us
    dot_general x1, local copies, waits for them, and re-layouts, per_device(): jnp.einsum('tsd,dc->tsc', selector, mode_taps, precision=highest)  6.16 us
  transfers between devices with their start and end apart: 2, of which 1 were waited for; matrix products, arithmetic and copies ran while one was open for 25% of the time, Pallas kernels for 0%

commit v1 on v0

--- a/solution.py
+++ b/solution.py
@@ -2,6 +2,7 @@
 import jax.numpy as jnp
 from jax import lax
 from jax.sharding import PartitionSpec as P
+from jax.lax import all_to_all, axis_size
 
 
 def passed_along(block, axis, distance):
@@ -82,7 +83,13 @@
         combine_blocks, (jnp.broadcast_to(block_decay[None], block_ends.shape), block_ends), axis=0
     )
     position = lax.axis_index("seq")
-    shard_rows = lax.all_gather(inclusive[-1:], "seq", axis=0, tiled=True)
+    unit = inclusive[-1:]
+    shard_rows = jnp.concatenate(
+        all_to_all(
+            jnp.stack(axis_size("seq") * [unit], 0), axis_name="seq", split_axis=0, concat_axis=0
+        ),
+        axis=0,
+    )
     owners = jnp.arange(shard_rows.shape[0], dtype=jnp.int32)
     distance = jnp.maximum(position - 1 - owners, 0).astype(jnp.float32)
     weight = jnp.where(

time: 194 us -> 206 us (1.062)
  the two profiles are of different devices: /device:TPU:16 before, /device:TPU:2 now
where the time goes in v1:
time: 206 us
  waiting for transfers between devices  66.9 us (32%)
  matrix products  50 us (24%)
  local copies, waits for them, and re-layouts  41.1 us (20%)
  blocking collectives  23.2 us (11%)
  starting transfers between devices  13.7 us (7%)
  other arithmetic  10.5 us (5%)
    all_to_all x1, waiting for transfers between devices, per_device(): all_to_all(jnp.stack(axis_size('seq') * [unit], 0), axis_name='seq', spli...  66.9 us
    psum x1, blocking collectives, per_device(): square_sum = lax.psum(local_squares, 'chan')  23.2 us
    dot_general x1, matrix products, per_device(): jnp.einsum('tnc,bnc->btc', decay_in, start_states, precision=highest)  17.5 us
    dot_general x1, matrix products, per_device(): jnp.einsum('tsc,bsc->btc', intra_block, blocks_in, precision=highest)  17.4 us
    another operation x2, local copies, waits for them, and re-layouts, band_matrix(): repeated = jnp.tile(padded, (filter_len, 1))[:filter_len * 2 * filter_len]  14 us
    all_to_all x1, starting transfers between devices, per_device(): all_to_all(jnp.stack(axis_size('seq') * [unit], 0), axis_name='seq', spli...  11.8 us
    dot_general x1, matrix products, per_device(): jnp.einsum('snc,bsc->bnc', decay_out, blocks_in, precision=highest)  11.1 us
    dot_general x1, local copies, waits for them, and re-layouts, per_device(): jnp.einsum('tsd,dc->tsc', selector, mode_taps, precision=highest)  6.15 us
  transfers between devices with their start and end apart: 2, of which 1 were waited for; matrix products, arithmetic and copies ran while one was open for 23% of the time, Pallas kernels for 0%

profile of v1, /device:TPU:2, one launch (start us, length us, event | category | flops | bytes accessed | tf_op | source)
XLA Modules:
  0.0 205.7 jit_solution(9429715464677841002)
XLA Ops:
  0.0 1.1 multiply_convert_fusion.2
  1.1 0.1 slice.93
  1.2 1.9 collective-permute-start
  3.1 0.8 rev.4
  3.9 0.1 pad.34.clone
  4.0 0.1 maximum_maximum_fusion
  4.1 0.2 copy.99
  4.3 3.2 %tile.4 = bf16[128,257,64]{1,0,2:T(8,128)(2,1)} broadcast(bf16[257,64]{0,1:T(8,128)(2,1)S(1)} %maximum_maximum_fusion), dimensions={1,2} | broadcast | bytes 4243584 | tf_op jit(solution)/shard_map/tile | solution.py:24
  7.5 10.8 %tile.10 = bf16[32896,64]{0,1:T(8,128)(2,1)} reshape(bf16[128,257,64]{1,0,2:T(8,128)(2,1)} %tile.4) | data formatting | bytes 8421376 | tf_op jit(solution)/shard_map/tile | solution.py:24
  18.3 0.0 slice-start
  18.3 2.2 %slice-done = bf16[32768,64]{0,1:T(8,128)(2,1)S(1)} async-done(((bf16[32896,64]{0,1:T(8,128)(2,1)}), bf16[32768,64]{0,1:T(8,128)(2,1)S(1)}, s32[]{:S(2)}) %slice-start) | async-done | bytes 4194328 | tf_op jit(solution)/shard_map/slice | solution.py:24
  20.5 0.0 copy-start
  20.5 0.0 copy-start.6
  20.5 3.0 %copy.113 = bf16[8,8,128,256]{3,2,1,0:T(8,128)(2,1)} copy(bf16[8,8,128,256]{3,1,2,0:T(8,128)(2,1)S(1)} %bitcast.49) | data formatting | bytes 8388608
  23.5 0.0 copy-done
  23.5 0.0 copy-start.4
  23.5 0.0 copy-start.5
  23.5 0.2 copy.102
  23.7 0.0 copy-done.6
  23.7 0.1 fusion.27
  23.8 0.0 collective-permute-done
  23.8 0.2 copy.112
  24.0 0.1 concatenate.18.clone
  24.1 3.4 %fusion.16 = f32[64,16,128]{2,1,0:T(8,128)S(1)} fusion(bf16[128,256,64]{1,0,2:T(8,128)(2,1)} %bitcast.50, bf16[1,128,64,16]{1,3,2,0:T(8,128)(2,1)S(1)} %bitcast.57, bf16[1,128,64,16]{1,3,2,0:T(8,128)(2,1)S(1)} %bitcast.56), kind=kOutput, calls=%fused_computation.20 | convolution fusion | flops 68157440 | bytes 5242880 | tf_op jit(solution)/shard_map/tsg,bsgk->btgk/dot_general | solution.py:35
  27.5 0.2 copy.100
  27.7 0.0 copy-done.4
  27.7 0.0 copy-done.5
  27.7 0.1 convert_multiply_fusion
  27.9 2.6 %copy.104 = f32[8,16,1024]{1,0,2:T(8,128)} copy(f32[8,16,1024]{2,1,0:T(8,128)S(1)} %bitcast.54) | data formatting | bytes 1048576 | tf_op jit(solution)/shard_map/reshape | solution.py:74
  30.5 11.1 %fusion.4 = f32[1024,8,16]{2,1,0:T(8,128)} fusion(f32[8,16,1024]{1,0,2:T(8,128)} %copy.104, f32[16]{0:T(128)S(1)} %subtract_negate_fusion, f32[16,1024]{0,1:T(8,128)S(1)} %copy.102), kind=kOutput, calls=%fused_computation.4 | convolution fusion | flops 25427968 | bytes 1114176 | tf_op jit(solution)/shard_map/snc,bsc->bnc/dot_general | solution.py:76
  41.6 2.8 %copy.107 = f32[1024,8,16]{0,2,1:T(8,128)S(1)} copy(f32[1024,8,16]{2,1,0:T(8,128)} %fusion.4) | data formatting | bytes 1048576 | tf_op jit(solution)/shard_map/snc,bsc->bnc/dot_general | solution.py:76
  44.6 0.0 copy-start.1
  44.7 0.1 pad.65
  44.7 2.5 %stack.2 = f32[64,1,16,1024]{3,2,1,0:T(8,128)} broadcast(f32[16,1024]{1,0:T(8,128)S(1)} %add_bitcast_fusion.1), dimensions={2,3} | broadcast | bytes 4259840 | tf_op jit(solution)/shard_map/stack | solution.py:89
  47.2 0.0 copy-done.1
  47.2 11.8 %all-to-all-start = ((f32[64,1,16,1024]{3,2,1,0:T(8,128)}), f32[64,1,16,1024]{3,2,1,0:T(8,128)}, u32[]{:S(2)}, u32[]{:S(2)}) async-start(f32[64,1,16,1024]{3,2,1,0:T(8,128)} %stack.2), calls=%async_computation | async-start | bytes 8388608 | tf_op jit(solution)/shard_map/all_to_all | solution.py:88
  59.0 0.2 copy.101
  59.2 3.5 %multiply_reduce_fusion = f32[16,1024]{0,1:T(8,128)S(1)} fusion(f32[16,1024]{0,1:T(8,128)S(1)} %copy.102, f32[16]{0:T(128)S(1)} %convert_negate_fusion, f32[16,1024]{0,1:T(8,128)S(1)} %copy.101), kind=kLoop, calls=%fused_computation.7 | loop fusion | flops 770048 | bytes 196672 | tf_op jit(solution)/shard_map/reduce_sum | solution.py:67
  62.7 0.6 fusion.19
  63.4 6.2 %copy.105 = f32[16,16,1024]{1,0,2:T(8,128)} copy(f32[16,16,1024]{2,1,0:T(8,128)S(1)} %fusion.19) | data formatting | bytes 2097152 | tf_op jit(solution)/shard_map/tsd,dc->tsc/dot_general | solution.py:71
  69.5 0.1 pad.26
  69.6 1.0 fusion.21
  70.6 0.1 pad.25
  70.7 0.1 slice_add_fusion
  70.8 17.4 %fusion.30 = f32[1024,8,16]{2,1,0:T(8,128)} fusion(f32[8,16,1024]{1,0,2:T(8,128)} %copy.104, f32[16,16,1024]{1,0,2:T(8,128)} %copy.105), kind=kOutput, calls=%fused_computation.64 | convolution fusion | flops 25165824 | bytes 2097152 | tf_op jit(solution)/shard_map/tsc,bsc->btc/dot_general | solution.py:75
  88.2 66.9 %all-to-all-done = f32[64,1,16,1024]{3,2,1,0:T(8,128)} async-done(((f32[64,1,16,1024]{3,2,1,0:T(8,128)}), f32[64,1,16,1024]{3,2,1,0:T(8,128)}, u32[]{:S(2)}, u32[]{:S(2)}) %all-to-all-start) | async-done | bytes 4194336 | tf_op jit(solution)/shard_map/all_to_all | solution.py:88
  155.1 3.1 %fusion.7 = f32[16,1024]{1,0:T(8,128)S(1)} fusion(f32[64,1,16,1024]{3,2,1,0:T(8,128)} %all-to-all-done, f32[16,1024]{1,0:T(8,128)S(1)} %copy-done, f32[64]{0:T(128)S(1)} %multiply_negate_fusion, pred[64]{0:T(512)(128)(4,1)S(1)} %iota_compare_fusion.2), kind=kLoop, calls=%fused_computation.9 | loop fusion | flops 4177920 | bytes 4325696 | tf_op jit(solution)/shard_map/reduce_sum | solution.py:100
  158.3 0.2 multiply_add_fusion
  158.4 2.6 %copy.108 = f32[8,16,1024]{1,0,2:T(8,128)} copy(f32[8,16,1024]{2,1,0:T(8,128)S(1)} %multiply_add_fusion) | data formatting | bytes 1048576 | tf_op jit(solution)/shard_map/add | solution.py:103
  161.0 17.5 %add_bitcast_fusion = f32[8,16,1024]{1,0,2:T(8,128)} fusion(f32[1024,8,16]{2,1,0:T(8,128)} %fusion.30, f32[8,16,1024]{1,0,2:T(8,128)} %copy.108, f32[16]{0:T(128)S(1)} %add_negate_fusion, f32[16,1024]{0,1:T(8,128)S(1)} %copy.102, f32[16,1024]{0,1:T(8,128)S(1)} %copy.101), kind=kOutput, calls=%fused_computation.10 | convolution fusion | flops 25821184 | bytes 1704000 | tf_op jit(solution)/shard_map/tnc,bnc->btc/dot_general | solution.py:106
  178.5 0.0 copy-start.2
  178.5 0.0 copy-start.3
  178.5 0.0 copy-start.7
  178.5 2.9 %copy.109 = f32[8,16,1024]{2,1,0:T(8,128)S(1)} copy(f32[8,16,1024]{1,0,2:T(8,128)} %add_bitcast_fusion) | data formatting | bytes 1048576 | tf_op jit(solution)/shard_map/add | solution.py:107
  181.4 0.0 copy-done.2
  181.4 0.0 copy-done.3
  181.4 0.2 multiply_reduce_fusion.1
  181.6 23.2 %psum.7 = f32[128]{0:T(128)S(1)} all-reduce(f32[128]{0:T(128)S(1)} %multiply_reduce_fusion.1), channel_id=1, replica_groups=mesh['seq'=64,'chan'=8] {'chan'}, use_global_device_ids=true, to_apply=%region_3.4 | all-reduce | flops 128 | bytes 1024 | tf_op jit(solution)/shard_map/psum | solution.py:114
  204.8 0.0 copy-done.7
  204.8 0.9 multiply_convert_fusion
  (22 shorter events, 0.3 us)
Async XLA Ops:
  1.2 22.6 %collective-permute-start = (bf16[127,1024]{1,0:T(8,128)(2,1)S(1)}, bf16[127,1024]{1,0:T(8,128)(2,1)S(1)}, u32[]{:S(2)}, u32[]{:S(2)}) collective-permute-start(bf16[127,1024]{1,0:T(8,128)(2,1)S(1)} %slice.93), channel_id=1, source_target_pairs={{0,8},{8,16},{16,24},{24,32},{32,40},{40,48},{48,56},{56,64},{64,7... | collective-permute-start | bytes 780296 | tf_op jit(solution)/shard_map/ppermute | solution.py:11
  18.3 2.2 %slice-start = ((bf16[32896,64]{0,1:T(8,128)(2,1)}), bf16[32768,64]{0,1:T(8,128)(2,1)S(1)}, s32[]{:S(2)}) async-start(bf16[32896,64]{0,1:T(8,128)(2,1)} %tile.10), calls=%async_computation.1 | async-start | bytes 8388608 | tf_op jit(solution)/shard_map/slice | solution.py:24
  20.5 3.0 %copy-start = (f32[16,1024]{1,0:T(8,128)S(1)}, f32[16,1024]{1,0:T(8,128)}, u32[]{:S(2)}) copy-start(f32[16,1024]{1,0:T(8,128)} %param.17) | copy-start | bytes 196612
  20.5 3.2 %copy-start.6 = (f32[16,1024]{1,0:T(8,128)S(1)}, f32[16,1024]{1,0:T(8,128)}, u32[]{:S(2)}) copy-start(f32[16,1024]{1,0:T(8,128)} %param.18) | copy-start | bytes 196612
  23.5 4.2 %copy-start.4 = (bf16[128,1024]{1,0:T(8,128)(2,1)S(1)}, bf16[128,1024]{1,0:T(8,128)(2,1)}, u32[]{:S(2)}) copy-start(bf16[128,1024]{1,0:T(8,128)(2,1)} %param.15) | copy-start | bytes 786436
  23.5 4.2 %copy-start.5 = (bf16[128,1024]{1,0:T(8,128)(2,1)S(1)}, bf16[128,1024]{1,0:T(8,128)(2,1)}, u32[]{:S(2)}) copy-start(bf16[128,1024]{1,0:T(8,128)(2,1)} %param.11) | copy-start | bytes 786436
  44.6 2.6 %copy-start.1 = (f32[4,16,1024]{2,1,0:T(8,128)}, f32[4,16,1024]{2,1,0:T(8,128)S(1)}, u32[]{:S(2)}) copy-start(f32[4,16,1024]{2,1,0:T(8,128)S(1)} %pad.24) | copy-start | bytes 786436
  47.2 107.9 %all-to-all-start = ((f32[64,1,16,1024]{3,2,1,0:T(8,128)}), f32[64,1,16,1024]{3,2,1,0:T(8,128)}, u32[]{:S(2)}, u32[]{:S(2)}) async-start(f32[64,1,16,1024]{3,2,1,0:T(8,128)} %stack.2), calls=%async_computation | async-start | bytes 8388608 | tf_op jit(solution)/shard_map/all_to_all | solution.py:88
  178.5 2.9 %copy-start.2 = (bf16[128,1024]{1,0:T(8,128)(2,1)S(1)}, bf16[128,1024]{1,0:T(8,128)(2,1)}, u32[]{:S(2)}) copy-start(bf16[128,1024]{1,0:T(8,128)(2,1)} %param.14) | copy-start | bytes 786436
  178.5 2.9 %copy-start.3 = (bf16[128,1024]{1,0:T(8,128)(2,1)S(1)}, bf16[128,1024]{1,0:T(8,128)(2,1)}, u32[]{:S(2)}) copy-start(bf16[128,1024]{1,0:T(8,128)(2,1)} %param.10) | copy-start | bytes 786436
  178.5 26.3 %copy-start.7 = (f32[1024]{0:T(1024)S(1)}, f32[1024]{0:T(1024)}, u32[]{:S(2)}) copy-start(f32[1024]{0:T(1024)} %param.19) | copy-start | bytes 12292
